TPU v7x, 256 devices: a whole 4x4x8 slice. The times are simulated.
256 devices in a mesh: dp: 16 (over x_lo, y, core), axial: 16 (over z, x_hi).
Axes of the slice: x: 4 (x_hi: 2, x_lo: 2; x = x_hi * 2 + x_lo), y: 4, z: 8, core: 2. Of those that a mesh axis runs over, the one named last changes fastest.
Arguments:
- homolog_activity: bfloat16 [512, 128, 256], P(('dp', 'axial')), parts along dimension 0, may hold values from -6 to 6
- homolog_symbol_ids: int32 [512, 128], P(('dp', 'axial')), parts along dimension 0, may hold values from 0 to 22
- residue_present_mask: int32 [2048], P('dp'), parts along dimension 0, may hold values 0 or 1
- pair_state: bfloat16 [2048, 128, 128], P(('dp', 'axial')), parts along dimension 0, may hold values from -6 to 6
- pair_valid_mask: int32 [2048, 128], P(('dp', 'axial')), parts along dimension 0, may hold values 0 or 1
- symbol_lookup_matrix: bfloat16 [23, 256], replicated, may hold values from -3 to 3
- row_query_weight: bfloat16 [256, 256], replicated, as said below
- horizontal_attention_matrix: bfloat16 [256, 768], replicated, may hold values from -0.375 to 0.375
- pair_bias_weight: bfloat16 [128, 8], replicated, may hold values from -0.5 to 0.5
- horizontal_final_matrix: bfloat16 [256, 256], replicated, may hold values from -0.375 to 0.375
- column_query_weight: bfloat16 [256, 256], replicated, as said below
- vertical_attention_matrix: bfloat16 [256, 768], replicated, may hold values from -0.375 to 0.375
- vertical_final_matrix: bfloat16 [256, 256], replicated, may hold values from -0.375 to 0.375
- tensor_mean_lift_matrix: bfloat16 [256, 64], replicated, may hold values from -0.375 to 0.375
- outer_product_output_weight: bfloat16 [1024, 128], replicated, may hold values from -0.75 to 0.75
- triangle_projection_weight: bfloat16 [128, 256], replicated, may hold values from -0.5 to 0.5
- triangle_projection_gate: bfloat16 [128, 256], replicated, may hold values from -0.5 to 0.5
- triangle_output_gate: bfloat16 [128, 128], replicated, may hold values from -0.5 to 0.5
- triangle_output_weight: bfloat16 [128, 128], replicated, may hold values from -0.5 to 0.5
Outputs:
- alignment_output: bfloat16 [512, 128, 256], P('dp', 'axial'), parts along dimension 0
- pair_output: bfloat16 [2048, 128, 128], P(('dp', 'axial')), parts along dimension 0
There are 16 independent parts, one for each index of `dp`. A program takes and returns all parts, laid end to end along the dimension named above; an argument that names none is the same for every part. Nothing has to cross between parts.
Inputs may be any that keep to these rules, and one draw needn't show every extreme that they name: `row_query_weight`: a projection of 256 inputs. `column_query_weight`: a projection of 256 inputs.
All inputs are finite; a program needn't handle non-finite values. No bound on the sum of `pair_valid_mask` on one device may be relied on, other than what follows from the above.
Results may differ from a plain program's by a relative error of at most 0.03.
The roundings to bfloat16 on the way count: a program that leaves them out, or rounds other values in their place, can miss the bound.
Values may be sent and summed in bfloat16 or wider, within the bound.
A program may use at most 64 MiB of HBM per device.

v0:
```python
import jax
import jax.numpy as jnp
from jax import lax
from jax.sharding import PartitionSpec as P

FOCUS_TOTAL = 8
FOCUS_SIZE = 32
MEAN_HIDDEN_SIZE = 32
C_TRI = 128


def layer_normalize(attended_entries):
    attended_entries = attended_entries.astype(jnp.float32)
    mean = jnp.mean(attended_entries, axis=-1, keepdims=True)
    centred = attended_entries - mean
    var = jnp.mean(centred * centred, axis=-1, keepdims=True)
    return centred * lax.rsqrt(var + 1e-05)


def gated_attend(evoformer_block, extra_axes, w_query, w_kvg, w_out):
    lines_list, residue_length, input_width = evoformer_block.shape
    width = FOCUS_TOTAL * FOCUS_SIZE
    flat = (
        layer_normalize(evoformer_block)
        .astype(jnp.bfloat16)
        .reshape(lines_list * residue_length, input_width)
    )
    query = (
        jnp.dot(flat, w_query, preferred_element_type=jnp.float32) * FOCUS_SIZE ** (-0.5)
    ).astype(jnp.bfloat16)
    query = query.reshape(lines_list, residue_length, FOCUS_TOTAL, FOCUS_SIZE)
    kvg = jnp.dot(flat, w_kvg, preferred_element_type=jnp.float32)
    keys = (
        kvg[:, :width]
        .astype(jnp.bfloat16)
        .reshape(lines_list, residue_length, FOCUS_TOTAL, FOCUS_SIZE)
    )
    attended_entries = (
        kvg[:, width : 2 * width]
        .astype(jnp.bfloat16)
        .reshape(lines_list, residue_length, FOCUS_TOTAL, FOCUS_SIZE)
    )
    gate = jax.nn.sigmoid(kvg[:, 2 * width :]).reshape(
        lines_list, residue_length, FOCUS_TOTAL, FOCUS_SIZE
    )
    scores = (
        jnp.einsum("bihd,bjhd->bhij", query, keys, preferred_element_type=jnp.float32) + extra_axes
    )
    top = jnp.max(scores, axis=-1, keepdims=True)
    expo = jnp.exp(scores - top)
    weights = (expo / jnp.sum(expo, axis=-1, keepdims=True)).astype(jnp.bfloat16)
    mixed = jnp.einsum(
        "bhij,bjhd->bihd", weights, attended_entries, preferred_element_type=jnp.float32
    )
    mixed = (mixed * gate).astype(jnp.bfloat16).reshape(lines_list * residue_length, width)
    return evoformer_block + jnp.dot(mixed, w_out, preferred_element_type=jnp.float32).reshape(
        lines_list, residue_length, input_width
    )


def finish_sums(evoformer_block, triangle_output_weight):
    mixed = layer_normalize(jnp.transpose(evoformer_block, (1, 2, 0))).astype(jnp.bfloat16)
    return jnp.einsum(
        "ijc,cz->ijz", mixed, triangle_output_weight, preferred_element_type=jnp.float32
    )


def local(
    homolog_activity,
    homolog_symbol_ids,
    residue_present_mask,
    pair_state,
    pair_valid_mask,
    symbol_lookup_matrix,
    row_query_weight,
    horizontal_attention_matrix,
    pair_bias_weight,
    horizontal_final_matrix,
    column_query_weight,
    vertical_attention_matrix,
    vertical_final_matrix,
    tensor_mean_lift_matrix,
    outer_product_output_weight,
    triangle_projection_weight,
    triangle_projection_gate,
    triangle_output_gate,
    triangle_output_weight,
):
    sequence_per_device, residue_length, input_width = homolog_activity.shape
    res_dev = pair_state.shape[0]
    group_size = lax.axis_size("axial")
    token_classes = symbol_lookup_matrix.shape[0]
    token_one_hot = (
        homolog_symbol_ids[..., None] == jnp.arange(token_classes, dtype=jnp.int32)
    ).astype(jnp.bfloat16)
    token_embedded = jnp.einsum(
        "slt,tc->slc", token_one_hot, symbol_lookup_matrix, preferred_element_type=jnp.float32
    )
    homolog_starting = homolog_activity.astype(jnp.float32) + token_embedded
    pair_norm = layer_normalize(pair_state).astype(jnp.bfloat16)
    bias_rows = jnp.einsum(
        "ijc,ch->hij", pair_norm, pair_bias_weight, preferred_element_type=jnp.float32
    ).astype(jnp.bfloat16)
    bias_full = lax.all_gather(bias_rows, "axial", axis=1, tiled=True)
    key_bias = 1000000000.0 * (residue_present_mask.astype(jnp.float32) - 1.0)
    extra_axes = bias_full.astype(jnp.float32)[None] + key_bias[None, None, None, :]
    cluster_total = homolog_starting.reshape(
        sequence_per_device // 2, 2, residue_length, input_width
    )
    homolog_across_update = lax.map(
        lambda evoformer_block: gated_attend(
            evoformer_block,
            extra_axes,
            row_query_weight,
            horizontal_attention_matrix,
            horizontal_final_matrix,
        ),
        cluster_total,
    )
    homolog_across_update = homolog_across_update.reshape(
        sequence_per_device, group_size, res_dev, input_width
    ).astype(jnp.bfloat16)
    moved = jnp.swapaxes(
        lax.all_to_all(homolog_across_update, "axial", split_axis=1, concat_axis=0, tiled=True)[
            :, 0
        ],
        0,
        1,
    )
    finished = lax.map(
        lambda item: gated_attend(
            item[None].astype(jnp.float32),
            0.0,
            column_query_weight,
            vertical_attention_matrix,
            vertical_final_matrix,
        )[0],
        moved,
    )
    exchanged = jnp.swapaxes(finished, 0, 1).astype(jnp.bfloat16)[:, None]
    sequence_count = exchanged.shape[0]
    alignment_after_columns = exchanged.reshape(sequence_count, res_dev, input_width)
    tensor_mean_scaler = layer_normalize(alignment_after_columns).astype(jnp.bfloat16)
    split_parts = jnp.einsum(
        "src,cf->rsf",
        tensor_mean_scaler,
        tensor_mean_lift_matrix,
        preferred_element_type=jnp.float32,
    ).astype(jnp.bfloat16)
    first_factor = split_parts[..., :MEAN_HIDDEN_SIZE]
    second_factor = split_parts[..., MEAN_HIDDEN_SIZE:].reshape(
        res_dev, sequence_count * MEAN_HIDDEN_SIZE
    )
    step_rows = 8
    left_blocks = first_factor.reshape(
        res_dev // step_rows, step_rows, sequence_count, MEAN_HIDDEN_SIZE
    )
    piece = lax.all_gather(second_factor, "axial", axis=0, tiled=True)
    count = piece.shape[0]
    right_part = piece.reshape(count, sequence_count, MEAN_HIDDEN_SIZE)

    def one_block(lines_list):
        tensor_mean = (
            jnp.einsum("isc,jsd->ijcd", lines_list, right_part, preferred_element_type=jnp.float32)
            / sequence_count
        )
        tensor_mean = tensor_mean.reshape(
            step_rows, count, MEAN_HIDDEN_SIZE * MEAN_HIDDEN_SIZE
        ).astype(jnp.bfloat16)
        return jnp.einsum(
            "ijf,fz->ijz",
            tensor_mean,
            outer_product_output_weight,
            preferred_element_type=jnp.float32,
        )

    update = lax.map(one_block, left_blocks).reshape(
        res_dev, count, outer_product_output_weight.shape[1]
    )
    pair_one = pair_state.astype(jnp.float32) + update
    tri_norm = layer_normalize(pair_one).astype(jnp.bfloat16)
    proj = jnp.einsum(
        "ikc,cf->fik", tri_norm, triangle_projection_weight, preferred_element_type=jnp.float32
    )
    gates = jnp.einsum(
        "ikc,cf->fik", tri_norm, triangle_projection_gate, preferred_element_type=jnp.float32
    )
    both = (jax.nn.sigmoid(gates) * proj * pair_valid_mask.astype(jnp.float32)[None]).astype(
        jnp.bfloat16
    )
    left_tri = both[:C_TRI]
    right_tri = both[C_TRI:]
    moved_left, moved_right = (
        lax.all_to_all(left_tri, "axial", split_axis=0, concat_axis=1, tiled=True),
        lax.all_to_all(right_tri, "axial", split_axis=0, concat_axis=1, tiled=True),
    )
    partial_sum = jnp.einsum(
        "cik,cjk->cij", moved_left, moved_right, preferred_element_type=jnp.float32
    )
    tri_sum = lax.all_to_all(
        partial_sum.astype(jnp.bfloat16), "axial", split_axis=1, concat_axis=0, tiled=True
    ).astype(partial_sum.dtype)
    tri_update = finish_sums(tri_sum, triangle_output_weight)
    out_gate = jax.nn.sigmoid(
        jnp.einsum(
            "ijc,cz->ijz", tri_norm, triangle_output_gate, preferred_element_type=jnp.float32
        )
    )
    pair_output = (pair_one + out_gate * tri_update).astype(jnp.bfloat16)
    return (alignment_after_columns, pair_output)


def solution(mesh):
    return jax.shard_map(
        local,
        mesh=mesh,
        in_specs=(
            P(("dp", "axial"), None, None),
            P(("dp", "axial"), None),
            P("dp"),
            P(("dp", "axial"), None, None),
            P(("dp", "axial"), None),
            P(),
            P(),
            P(),
            P(),
            P(),
            P(),
            P(),
            P(),
            P(),
            P(),
            P(),
            P(),
            P(),
            P(),
        ),
        out_specs=(P("dp", "axial", None), P(("dp", "axial"), None, None)),
        check_vma=False,
    )
```

profile of v0, /device:TPU:16, one launch (start us, length us, event | category | flops | bytes accessed | tf_op | source)
XLA Modules:
  0.0 182.2 jit_solution(16834512736423515451)
XLA Ops:
  0.7 1.2 copy.137
  2.0 0.9 fusion.49
  2.9 45.2 %all_gather.6 = bf16[8,128,128]{2,0,1:T(8,128)(2,1)S(1)} all-gather(bf16[8,8,128]{2,0,1:T(8,128)(2,1)S(1)} %fusion.49), channel_id=1, replica_groups=mesh['dp'=16,'axial'=16] {'axial'}, dimensions={1}, use_global_device_ids=true | all-gather | bytes 278528 | tf_op jit(solution)/shard_map/all_gather | solution.py:104
  48.1 0.7 add_multiply_fusion
  49.1 0.3 fusion.103
  50.1 0.7 fusion.101
  51.2 0.4 convolution_add_fusion
  51.6 0.5 fusion.105
  52.1 1.0 copy.132
  53.6 0.4 fusion.45
  53.9 0.5 copy-done.7
  54.6 0.7 copy.145
  55.3 3.5 %all-to-all-start = ((bf16[2,16,8,256]{3,2,0,1:T(8,128)(2,1)}), bf16[2,16,8,256]{3,2,0,1:T(8,128)(2,1)S(1)}, u32[]{:S(2)}, u32[]{:S(2)}) async-start(bf16[2,16,8,256]{3,2,0,1:T(8,128)(2,1)} %copy.145), calls=%async_computation | async-start | bytes 262144 | tf_op jit(solution)/shard_map/all_to_all | solution.py:124
  58.9 11.1 %all-to-all-done = bf16[2,16,8,256]{3,2,0,1:T(8,128)(2,1)S(1)} async-done(((bf16[2,16,8,256]{3,2,0,1:T(8,128)(2,1)}), bf16[2,16,8,256]{3,2,0,1:T(8,128)(2,1)S(1)}, u32[]{:S(2)}, u32[]{:S(2)}) %all-to-all-start) | async-done | bytes 131104 | tf_op jit(solution)/shard_map/all_to_all | solution.py:124
  70.1 17.2 %while.2 = (s32[]{:T(128)}, bf16[8,32,256]{2,0,1:T(8,128)(2,1)S(1)}, bf16[8,32,256]{2,1,0:T(8,128)(2,1)S(1)}, bf16[256,768]{1,0:T(8,128)(2,1)S(1)}, bf16[256,256...) while((s32[]{:T(128)}, bf16[8,32,256]{2,0,1:T(8,128)(2,1)S(1)}, ...), condition=%wide.region_11.12_spmd, body=%wide.region_6.11_spmd.sunk | while | flops 22806880 | bytes 1496045 | solution.py:130
  88.1 37.6 %all_gather.7 = bf16[128,1024]{1,0:T(8,128)(2,1)S(1)} all-gather(bf16[8,1024]{1,0:T(8,128)(2,1)S(1)} %reshape.196), channel_id=1, replica_groups=mesh['dp'=16,'axial'=16] {'axial'}, dimensions={0}, use_global_device_ids=true | all-gather | bytes 278528 | tf_op jit(solution)/shard_map/all_gather | solution.py:158
  126.0 0.7 fusion.28
  126.7 1.4 copy.152
  128.1 0.5 fusion.110
  128.9 0.3 fusion.78
  129.5 0.5 fusion.37
  130.1 0.9 copy.159
  131.0 4.6 %all-to-all-start.1 = ((bf16[128,8,128]{2,1,0:T(8,128)(2,1)}), bf16[128,8,128]{2,1,0:T(8,128)(2,1)S(1)}, u32[]{:S(2)}, u32[]{:S(2)}) async-start(bf16[128,8,128]{2,1,0:T(8,128)(2,1)} %copy.159), calls=%async_computation.1 | async-start | bytes 524288 | tf_op jit(solution)/shard_map/all_to_all | solution.py:194
  135.8 12.4 %all-to-all-done.1 = bf16[128,8,128]{2,1,0:T(8,128)(2,1)S(1)} async-done(((bf16[128,8,128]{2,1,0:T(8,128)(2,1)}), bf16[128,8,128]{2,1,0:T(8,128)(2,1)S(1)}, u32[]{:S(2)}, u32[]{:S(2)}) %all-to-all-start.1) | async-done | bytes 262176 | tf_op jit(solution)/shard_map/all_to_all | solution.py:194
  148.2 15.5 %all_to_all.60 = bf16[128,8,128]{2,1,0:T(8,128)(2,1)S(1)} all-to-all(bf16[128,8,128]{2,1,0:T(8,128)(2,1)S(1)} %copy.161), channel_id=1, replica_groups=mesh['dp'=16,'axial'=16] {'axial'}, dimensions={0} | all-to-all | bytes 524288 | tf_op jit(solution)/shard_map/all_to_all | solution.py:195
  163.7 0.3 convolution_convert_fusion
  164.0 0.9 copy.163
  164.8 3.5 %all-to-all-start.3 = ((bf16[8,128,128]{2,0,1:T(8,128)(2,1)}), bf16[8,128,128]{2,0,1:T(8,128)(2,1)S(1)}, u32[]{:S(2)}, u32[]{:S(2)}) async-start(bf16[8,128,128]{2,0,1:T(8,128)(2,1)} %copy.163), calls=%async_computation.3 | async-start | bytes 524288 | tf_op jit(solution)/shard_map/all_to_all | solution.py:200
  168.4 0.3 fusion.40
  168.8 11.8 %all-to-all-done.3 = bf16[8,128,128]{2,0,1:T(8,128)(2,1)S(1)} async-done(((bf16[8,128,128]{2,0,1:T(8,128)(2,1)}), bf16[8,128,128]{2,0,1:T(8,128)(2,1)S(1)}, u32[]{:S(2)}, u32[]{:S(2)}) %all-to-all-start.3) | async-done | bytes 262176 | tf_op jit(solution)/shard_map/all_to_all | solution.py:200
  181.1 0.3 fusion.42
  181.3 0.9 copy.168
  (224 shorter events, 21.2 us)
Async XLA Ops:
  0.6 49.1 %copy-start = (bf16[256,768]{1,0:T(8,128)(2,1)S(1)}, bf16[256,768]{1,0:T(8,128)(2,1)}, u32[]{:S(2)}) copy-start(bf16[256,768]{1,0:T(8,128)(2,1)} %param.28) | copy-start | bytes 1179652
  0.6 48.4 %copy-start.5 = (bf16[2,128,256]{2,1,0:T(8,128)(2,1)S(1)}, bf16[2,128,256]{2,1,0:T(8,128)(2,1)}, u32[]{:S(2)}) copy-start(bf16[2,128,256]{2,1,0:T(8,128)(2,1)} %param.21) | copy-start | bytes 393220
  0.7 48.4 %copy-start.12 = (s32[2,128]{1,0:T(2,128)S(1)}, s32[2,128]{1,0:T(2,128)}, u32[]{:S(2)}) copy-start(s32[2,128]{1,0:T(2,128)} %param.22) | copy-start | bytes 3076
  0.7 48.4 %copy-start.10 = (bf16[23,256]{1,0:T(8,128)(2,1)S(1)}, bf16[23,256]{1,0:T(8,128)(2,1)}, u32[]{:S(2)}) copy-start(bf16[23,256]{1,0:T(8,128)(2,1)} %param.26) | copy-start | bytes 35332
  49.1 1.8 copy-start.6
  53.5 0.9 copy-start.7
  53.5 5.3 %copy-start.11 = (s32[8,128]{1,0:T(8,128)S(1)}, s32[8,128]{1,0:T(8,128)}, u32[]{:S(2)}) copy-start(s32[8,128]{1,0:T(8,128)} %param.25) | copy-start | bytes 12292
  53.5 16.5 %copy-start.1 = (bf16[256,768]{1,0:T(8,128)(2,1)S(1)}, bf16[256,768]{1,0:T(8,128)(2,1)}, u32[]{:S(2)}) copy-start(bf16[256,768]{1,0:T(8,128)(2,1)} %param.32) | copy-start | bytes 1179652
  53.5 16.5 %copy-start.2 = (bf16[256,256]{1,0:T(8,128)(2,1)S(1)}, bf16[256,256]{1,0:T(8,128)(2,1)}, u32[]{:S(2)}) copy-start(bf16[256,256]{1,0:T(8,128)(2,1)} %param.33) | copy-start | bytes 393220
  53.6 16.5 %copy-start.13 = (bf16[256,256]{1,0:T(8,128)(2,1)S(1)}, bf16[256,256]{1,0:T(8,128)(2,1)}, u32[]{:S(2)}) copy-start(bf16[256,256]{1,0:T(8,128)(2,1)} %param.31) | copy-start | bytes 393220
  55.3 14.7 %all-to-all-start = ((bf16[2,16,8,256]{3,2,0,1:T(8,128)(2,1)}), bf16[2,16,8,256]{3,2,0,1:T(8,128)(2,1)S(1)}, u32[]{:S(2)}, u32[]{:S(2)}) async-start(bf16[2,16,8,256]{3,2,0,1:T(8,128)(2,1)} %copy.145), calls=%async_computation | async-start | bytes 262144 | tf_op jit(solution)/shard_map/all_to_all | solution.py:124
  70.1 17.6 %copy-start.15 = (bf16[256,64]{0,1:T(8,128)(2,1)S(1)}, bf16[256,64]{0,1:T(8,128)(2,1)}, u32[]{:S(2)}) copy-start(bf16[256,64]{0,1:T(8,128)(2,1)} %param.34) | copy-start | bytes 98308
  87.3 39.4 %copy-start.3 = (bf16[8,32,256]{2,0,1:T(8,128)(2,1)}, bf16[8,32,256]{2,0,1:T(8,128)(2,1)S(1)}, u32[]{:S(2)}) copy-start(bf16[8,32,256]{2,0,1:T(8,128)(2,1)S(1)} %get-tuple-element.65) | copy-start | bytes 393220
  126.7 1.4 copy-start.4
  128.1 0.8 copy-start.8
  128.6 0.8 copy-start.14
  130.1 38.3 %copy-start.16 = (bf16[128,128]{1,0:T(8,128)(2,1)S(1)}, bf16[128,128]{1,0:T(8,128)(2,1)}, u32[]{:S(2)}) copy-start(bf16[128,128]{1,0:T(8,128)(2,1)} %param.38) | copy-start | bytes 98308
  131.0 17.2 %all-to-all-start.1 = ((bf16[128,8,128]{2,1,0:T(8,128)(2,1)}), bf16[128,8,128]{2,1,0:T(8,128)(2,1)S(1)}, u32[]{:S(2)}, u32[]{:S(2)}) async-start(bf16[128,8,128]{2,1,0:T(8,128)(2,1)} %copy.159), calls=%async_computation.1 | async-start | bytes 524288 | tf_op jit(solution)/shard_map/all_to_all | solution.py:194
  164.8 15.8 %all-to-all-start.3 = ((bf16[8,128,128]{2,0,1:T(8,128)(2,1)}), bf16[8,128,128]{2,0,1:T(8,128)(2,1)S(1)}, u32[]{:S(2)}, u32[]{:S(2)}) async-start(bf16[8,128,128]{2,0,1:T(8,128)(2,1)} %copy.163), calls=%async_computation.3 | async-start | bytes 524288 | tf_op jit(solution)/shard_map/all_to_all | solution.py:200
  168.7 12.3 %copy-start.9 = (bf16[128,128]{1,0:T(8,128)(2,1)S(1)}, bf16[128,128]{1,0:T(8,128)(2,1)}, u32[]{:S(2)}) copy-start(bf16[128,128]{1,0:T(8,128)(2,1)} %param.39) | copy-start | bytes 98308
where the time goes:
time: 183 us; the launch traced here: 182 us
  blocking collectives  98.3 us (54%)
  waiting for transfers between devices  35.4 us (19%)
  local copies, waits for them, and re-layouts  15.2 us (8%)
  matrix products  15.1 us (8%)
  starting transfers between devices  11.6 us (6%)
  other arithmetic  4.74 us (3%)
    all_gather x1, blocking collectives, local(): bias_full = lax.all_gather(bias_rows, 'axial', axis=1, tiled=True)  45.2 us
    all_gather x1, blocking collectives, local(): piece = lax.all_gather(second_factor, 'axial', axis=0, tiled=True)  37.6 us
    all_to_all x1, blocking collectives, local(): lax.all_to_all(right_tri, 'axial', split_axis=0, concat_axis=1, tiled=True)  15.5 us
    all_to_all x1, waiting for transfers between devices, local(): lax.all_to_all(left_tri, 'axial', split_axis=0, concat_axis=1, tiled=True)  12.4 us
    all_to_all x1, waiting for transfers between devices, local(): lax.all_to_all(partial_sum.astype(jnp.bfloat16), 'axial', split_axis=1, c...  11.8 us
    all_to_all x1, waiting for transfers between devices, local(): lax.all_to_all(homolog_across_update, 'axial', split_axis=1, concat_axis=...  11.1 us
    all_to_all x1, starting transfers between devices, local(): lax.all_to_all(left_tri, 'axial', split_axis=0, concat_axis=1, tiled=True)  4.6 us
  transfers between devices with their start and end apart: 3, of which 3 were waited for; matrix products, arithmetic and copies ran while one was open for 0% of the time, Pallas kernels for 0%

commit v1 on v0

v1 whole, which is shorter than its diff:
```python
import jax
import jax.numpy as jnp
from jax import lax
from jax.experimental import pallas as pl
from jax.experimental.pallas import tpu as pltpu
from jax.sharding import PartitionSpec as P

N = 16
HEADS = 8
HEAD = 32
F32 = jnp.float32
BF16 = jnp.bfloat16
NN = (((1,), (0,)), ((), ()))
NT = (((1,), (1,)), ((), ()))
TN = (((0,), (0,)), ((), ()))

BIAS, MSA, OPM, TRI, SUM = range(5)


def dot(a, b, dims=NN):
    return lax.dot_general(a, b, dims, preferred_element_type=F32)


def sigmoid(x):
    return 1.0 / (1.0 + jnp.exp(-x))


def norm(x, axis=-1):
    centred = x - jnp.mean(x, axis=axis, keepdims=True)
    var = jnp.mean(centred * centred, axis=axis, keepdims=True)
    return (centred * lax.rsqrt(var + 1e-05)).astype(BF16)


def kernel(
    act, ids, present, pair, valid, table,
    row_q, row_kvg, bias_w, row_o, col_q, col_kvg, col_o,
    lift, opm_w, tri_w, tri_g, out_g, out_w,
    msa_out, pair_out,
    bias_send, bias_recv, msa_send, msa_recv, opm_send, opm_recv,
    tri_send, tri_recv, sum_send, sum_recv,
    bias_rows, bias_all, table_pad, xr, w2, wt, lift_x, opm_f, tcat,
    pair_one, tri_n, gate, xt, yt, zt,
    send_sem, recv_sem,
):
    me = lax.axis_index("axial")
    barrier = pltpu.get_barrier_semaphore()
    for r in range(1, N):
        pl.semaphore_signal(
            barrier, inc=1, device_id={"axial": lax.rem(me + r, N)},
            device_id_type=pl.DeviceIdType.MESH,
        )

    def copy(phase, r, src, dst):
        return pltpu.make_async_remote_copy(
            src_ref=src, dst_ref=dst,
            send_sem=send_sem.at[phase, r], recv_sem=recv_sem.at[phase, r],
            device_id={"axial": lax.rem(me + r, N)},
            device_id_type=pl.DeviceIdType.MESH,
        )

    def gather_copy(phase, r, send, recv):
        return copy(phase, r, send, recv.at[me])

    def scatter_copy(phase, r, send, recv):
        return copy(phase, r, send.at[lax.rem(me + r, N)], recv.at[me])

    def await_all(phase, recv):
        for r in range(1, N):
            src = lax.rem(me + (N - r), N)
            pltpu.make_async_remote_copy(
                src_ref=recv.at[src], dst_ref=recv.at[src],
                send_sem=send_sem.at[phase, r], recv_sem=recv_sem.at[phase, r],
                device_id={"axial": lax.rem(me + r, N)},
                device_id_type=pl.DeviceIdType.MESH,
            ).wait_recv()

    pn = norm(pair[...].astype(F32)).reshape(1024, 128)
    bias_t = dot(bias_w[...].astype(F32).T.astype(BF16), pn, NT)
    for i in range(8):
        bias_rows[pl.ds(i, 8, stride=8), :] = bias_t[:, i * 128:(i + 1) * 128]
    bias_send[...] = bias_rows[...].astype(BF16)
    bias_recv[me] = bias_rows[...].astype(BF16)

    pl.semaphore_wait(barrier, N - 1)
    for r in range(1, N):
        gather_copy(BIAS, r, bias_send, bias_recv).start()

    table_pad[...] = jnp.zeros((32, 256), F32)
    table_pad[0:23, :] = table[...].astype(F32)
    table_b = table_pad[...].astype(BF16)
    kinds = lax.broadcasted_iota(jnp.int32, (32, 128), 0)
    x_rows = []
    for s in range(2):
        hot = (kinds == ids[s:s + 1, :]).astype(F32).T.astype(BF16)
        x_rows.append(act[s].astype(F32) + dot(hot, table_b))
    x = jnp.concatenate(x_rows, axis=0)

    head_of = lax.broadcasted_iota(jnp.int32, (1, 256), 1) // HEAD
    head_mask = [(head_of == h).astype(F32).astype(BF16) for h in range(HEADS)]

    def project(x, wq, wkvg):
        xn = norm(x)
        q = (dot(xn, wq[...]) * HEAD ** -0.5).astype(BF16)
        kvg = dot(xn, wkvg[...])
        return q, kvg[:, :256].astype(BF16), kvg[:, 256:512].astype(BF16), kvg[:, 512:]

    def attend(q, k, v, g, extra):
        halves = []
        for s in range(2):
            rows = slice(s * 128, (s + 1) * 128)
            acc = jnp.zeros((128, 256), F32)
            for h in range(HEADS):
                scores = dot(q[rows] * head_mask[h], k[rows], NT) + extra(h)
                top = jnp.max(scores, axis=-1, keepdims=True)
                expo = jnp.exp(scores - top)
                total = jnp.sum(expo, axis=-1, keepdims=True)
                weights = (expo * (1.0 / total)).astype(BF16)
                mixed = dot(weights, v[rows])
                acc = jnp.where(head_of == h, mixed, acc)
            halves.append(acc)
        return (jnp.concatenate(halves, axis=0) * sigmoid(g)).astype(BF16)

    q, k, v, g = project(x, row_q, row_kvg)

    opm_f[...] = opm_w[...].astype(F32)
    for d in range(32):
        w2[:, d * 128:(d + 1) * 128] = opm_f[pl.ds(d, 32, stride=32), :].astype(BF16)
    wt[0:256, :] = tri_w[...].astype(F32).T.astype(BF16)
    wt[256:512, :] = tri_g[...].astype(F32).T.astype(BF16)
    spread = (
        lax.broadcasted_iota(jnp.int32, (64, 1024), 0)
        == 32 + lax.broadcasted_iota(jnp.int32, (64, 1024), 1) // 32
    ).astype(F32).astype(BF16)
    lift_x[...] = dot(lift[...], spread).astype(BF16)

    await_all(BIAS, bias_recv)
    key_bias = 1000000000.0 * (present[...].astype(F32) - 1.0)
    for p in range(N):
        block = bias_recv[p].astype(F32)
        for h in range(HEADS):
            bias_all[h, p * 8:(p + 1) * 8, :] = block[h * 8:(h + 1) * 8] + key_bias
    heads = attend(q, k, v, g, lambda h: bias_all[h])
    msa_one = x + dot(heads, row_o[...])
    for p in range(N):
        block = jnp.concatenate(
            [msa_one[p * 8:(p + 1) * 8], msa_one[128 + p * 8:128 + (p + 1) * 8]], axis=0
        )
        msa_send[p] = block.astype(BF16)
    msa_recv[me] = msa_send[me]
    for r in range(1, N):
        scatter_copy(MSA, r, msa_send, msa_recv).start()
    await_all(MSA, msa_recv)

    for p in range(N):
        block = msa_recv[p].astype(F32)
        for half in range(2):
            xr[half, p * 16:(p + 1) * 16, :] = block[:, half * 128:(half + 1) * 128]
    x = jnp.concatenate(
        [
            jnp.concatenate(
                [xr[half, pl.ds(l, 32, stride=8), :] for l in range(8)], axis=0
            )
            for half in range(2)
        ],
        axis=1,
    )
    q, k, v, g = project(x, col_q, col_kvg)
    own = jnp.where(
        lax.broadcasted_iota(jnp.int32, (128, 128), 0) // 32
        == lax.broadcasted_iota(jnp.int32, (128, 128), 1) // 32,
        0.0, -jnp.inf,
    ).astype(F32)
    heads = attend(q, k, v, g, lambda h: own)
    z = (x + dot(heads, col_o[...])).astype(BF16)

    zf = z.astype(F32)
    zn = norm(zf)
    right = dot(zn, lift_x[...])
    keep = (
        lax.broadcasted_iota(jnp.int32, (256, 1024), 0) % 32
        == lax.broadcasted_iota(jnp.int32, (256, 1024), 1) % 32
    )
    right = jnp.where(keep, right, 0.0).astype(BF16)
    pick = (
        lax.broadcasted_iota(jnp.int32, (8, 256), 0)
        == lax.broadcasted_iota(jnp.int32, (8, 256), 1) // 32
    ).astype(F32).astype(BF16)
    right = dot(pick, right)
    right = jnp.concatenate([right[:, :512], right[:, 512:]], axis=0).astype(BF16)
    opm_send[...] = right
    opm_recv[me] = right
    for r in range(1, N):
        gather_copy(OPM, r, opm_send, opm_recv).start()

    for half in range(2):
        for l in range(8):
            xr[half, pl.ds(l, 32, stride=8), :] = zf[
                l * 32:(l + 1) * 32, half * 128:(half + 1) * 128
            ]
    for half in range(2):
        msa_out[:, :, half * 128:(half + 1) * 128] = (
            xr[half].reshape(32, 8, 128).astype(BF16)
        )
    left = dot(zn, lift[...]).astype(BF16)[:, :32]
    for d in range(0, 32, 2):
        t = dot(left, w2[:, d * 128:(d + 2) * 128]).astype(BF16)
        for i in range(8):
            for e in range(2):
                tcat[(d + e) * 32:(d + e + 1) * 32, i * 128:(i + 1) * 128] = t[
                    i * 32:(i + 1) * 32, e * 128:(e + 1) * 128
                ]

    await_all(OPM, opm_recv)
    blocks = [opm_recv[p].astype(F32) for p in range(N)]
    right = jnp.concatenate(
        [
            jnp.concatenate([b[:8] for b in blocks], axis=0),
            jnp.concatenate([b[8:] for b in blocks], axis=0),
        ],
        axis=1,
    ).astype(BF16)

    for i in range(8):
        update = dot(right, tcat[:, i * 128:(i + 1) * 128])
        one = pair[i].astype(F32) + update * (1.0 / 32)
        pair_one[i] = one
        tn = norm(one)
        tri_n[i] = tn
        both = dot(wt[...], tn, NT)
        both = sigmoid(both[256:]) * both[:256] * valid[i:i + 1, :].astype(F32)
        for p in range(N):
            block = jnp.concatenate(
                [both[p * 8:(p + 1) * 8], both[128 + p * 8:128 + (p + 1) * 8]], axis=0
            )
            tri_send[p, :, i * 128:(i + 1) * 128] = block.astype(BF16)
    tri_recv[me] = tri_send[me]
    for r in range(1, N):
        scatter_copy(TRI, r, tri_send, tri_recv).start()
    for i in range(8):
        gate[i] = sigmoid(dot(tri_n[i], out_g[...]))
    await_all(TRI, tri_recv)

    for p in range(N):
        for i in range(8):
            at = (p * 8 + i) * 16
            xt[at:at + 16, :] = tri_recv[p, :, i * 128:(i + 1) * 128].astype(F32)
    for c in range(8):
        a = xt[pl.ds(c, 128, stride=16), :].astype(BF16)
        b = xt[pl.ds(8 + c, 128, stride=16), :].astype(BF16)
        yt[pl.ds(c, 128, stride=8), :] = dot(a, b, NT)
    for p in range(N):
        sum_send[p] = yt[p * 64:(p + 1) * 64, :].astype(BF16)
    sum_recv[me] = sum_send[me]
    for r in range(1, N):
        scatter_copy(SUM, r, sum_send, sum_recv).start()
    await_all(SUM, sum_recv)

    for p in range(N):
        block = sum_recv[p].astype(F32)
        for i in range(8):
            zt[i, p * 8:(p + 1) * 8, :] = block[i * 8:(i + 1) * 8]
    for i in range(8):
        mixed = norm(zt[i], axis=0)
        update = dot(mixed, out_w[...], TN)
        pair_out[i] = (pair_one[i] + gate[i] * update).astype(BF16)

    for r in range(1, N):
        gather_copy(BIAS, r, bias_send, bias_recv).wait_send()
        scatter_copy(MSA, r, msa_send, msa_recv).wait_send()
        gather_copy(OPM, r, opm_send, opm_recv).wait_send()
        scatter_copy(TRI, r, tri_send, tri_recv).wait_send()
        scatter_copy(SUM, r, sum_send, sum_recv).wait_send()


def local(act, ids, present, *rest):
    vmem = pl.BlockSpec(memory_space=pltpu.VMEM)
    args = (act, ids, present.reshape(1, 128), *rest)
    return pl.pallas_call(
        kernel,
        out_shape=(
            jax.ShapeDtypeStruct((32, 8, 256), BF16),
            jax.ShapeDtypeStruct((8, 128, 128), BF16),
        ),
        in_specs=[vmem] * len(args),
        out_specs=(vmem, vmem),
        scratch_shapes=[
            pltpu.VMEM((64, 128), BF16),
            pltpu.VMEM((N, 64, 128), BF16),
            pltpu.VMEM((N, 16, 256), BF16),
            pltpu.VMEM((N, 16, 256), BF16),
            pltpu.VMEM((16, 512), BF16),
            pltpu.VMEM((N, 16, 512), BF16),
            pltpu.VMEM((N, 16, 1024), BF16),
            pltpu.VMEM((N, 16, 1024), BF16),
            pltpu.VMEM((N, 64, 128), BF16),
            pltpu.VMEM((N, 64, 128), BF16),
            pltpu.VMEM((64, 128), F32),
            pltpu.VMEM((HEADS, 128, 128), F32),
            pltpu.VMEM((32, 256), F32),
            pltpu.VMEM((2, 256, 128), F32),
            pltpu.VMEM((32, 4096), BF16),
            pltpu.VMEM((512, 128), BF16),
            pltpu.VMEM((256, 1024), BF16),
            pltpu.VMEM((1024, 128), F32),
            pltpu.VMEM((1024, 1024), BF16),
            pltpu.VMEM((8, 128, 128), F32),
            pltpu.VMEM((8, 128, 128), BF16),
            pltpu.VMEM((8, 128, 128), F32),
            pltpu.VMEM((2048, 128), F32),
            pltpu.VMEM((1024, 128), F32),
            pltpu.VMEM((8, 128, 128), F32),
            pltpu.SemaphoreType.DMA((5, N)),
            pltpu.SemaphoreType.DMA((5, N)),
        ],
        compiler_params=pltpu.CompilerParams(
            collective_id=0, has_side_effects=True, vmem_limit_bytes=48 * 1024 * 1024,
        ),
        cost_estimate=pl.CostEstimate(flops=10**9, bytes_accessed=3 * 10**6, transcendentals=10**6),
    )(*args)


def solution(mesh):
    rows = P(("dp", "axial"))
    return jax.shard_map(
        local,
        mesh=mesh,
        in_specs=(rows, rows, P("dp"), rows, rows) + (P(),) * 14,
        out_specs=(P("dp", "axial", None), rows),
        check_vma=False,
    )
```

time: 183 us -> 81.5 us (0.45)
  blocking collectives: 98.3 us -> 0 us
  Pallas kernels: 0 us -> 64.9 us
  waiting for transfers between devices: 35.4 us -> 0 us
  matrix products: 15.1 us -> 0 us
  starting transfers between devices: 11.6 us -> 0 us
  other arithmetic: 4.74 us -> 0 us
    all_gather x2 -> x0, blocking collectives: 82.8 us -> none  [the longest x1 45.2 us: local(): bias_full = lax.all_gather(bias_rows, 'axial', axis=1, tiled=True)]
    pallas_call x0 -> x1, Pallas kernels: none -> 64.9 us  [local(): pl.pallas_call(kernel, out_shape=(jax.ShapeDtypeStruct((32, 8, 256), BF16...]
    all_to_all x3 -> x0, waiting for transfers between devices: 35.4 us -> none  [the longest x1 12.4 us: local(): lax.all_to_all(left_tri, 'axial', split_axis=0, concat_axis=1, tiled=True)]
    all_to_all x1 -> x0, blocking collectives: 15.5 us -> none  [local(): lax.all_to_all(right_tri, 'axial', split_axis=0, concat_axis=1, tiled=True)]
    dot_general x55 -> x0, matrix products: 13 us -> none  [the longest x9 2.14 us: gated_attend(): kvg = jnp.dot(flat, w_kvg, preferred_element_type=jnp.float32)]
    unnamed x36 -> x38, local copies, waits for them, and re-layouts: 2.95 us -> 15.2 us
    all_to_all x3 -> x0, starting transfers between devices: 11.6 us -> none  [the longest x1 4.6 us: local(): lax.all_to_all(left_tri, 'axial', split_axis=0, concat_axis=1, tiled=True)]
    reduce_sum x24 -> x0, other arithmetic: 3.32 us -> none  [the longest x13 2.12 us: layer_normalize(): var = jnp.mean(centred * centred, axis=-1, keepdims=True)]
  transfers between devices with their start and end apart: 3 -> 0, of which waited for: 3 -> 0; matrix products, arithmetic and copies ran while one was open for 0% -> 0% of each run, Pallas kernels for 0% -> 0%
where the time goes in v1:
time: 81.5 us; the launch traced here: 80.8 us
  Pallas kernels  64.9 us (80%)
  local copies, waits for them, and re-layouts  15.2 us (19%)
    pallas_call x1, Pallas kernels, local(): pl.pallas_call(kernel, out_shape=(jax.ShapeDtypeStruct((32, 8, 256), BF16...  64.9 us
    unnamed x38, local copies, waits for them, and re-layouts  15.2 us

profile of v1, /device:TPU:16, one launch (start us, length us, event | category | flops | bytes accessed | tf_op | source)
XLA Modules:
  0.0 80.8 jit_solution(15414316020736416218)
XLA Ops:
  0.6 0.0 copy-start.4
  0.6 0.8 %copy.21.bias_w = bf16[128,8]{1,0:T(8,128)(2,1)S(1)} copy(bf16[128,8]{0,1:T(8,128)(2,1)} %param.27) | data formatting | bytes 4096 | tf_op args[8]
  1.5 0.0 copy-start.15
  1.5 0.0 copy-start.16
  1.5 0.9 %copy.22.lift = bf16[256,64]{1,0:T(8,128)(2,1)S(1)} copy(bf16[256,64]{0,1:T(8,128)(2,1)} %param.32) | data formatting | bytes 65536 | tf_op args[13]
  2.4 0.0 copy-done.4
  2.4 0.0 copy-done.15
  2.4 0.0 copy-done.16
  2.4 0.0 copy-start
  2.4 1.0 %copy-done = bf16[256,768]{1,0:T(8,128)(2,1)S(1)} copy-done((bf16[256,768]{1,0:T(8,128)(2,1)S(1)}, bf16[256,768]{1,0:T(8,128)(2,1)}, u32[]{:S(2)}) %copy-start) | copy-done | bytes 393240
  3.4 0.0 copy-start.1
  3.4 1.0 %copy-done.1 = bf16[256,768]{1,0:T(8,128)(2,1)S(1)} copy-done((bf16[256,768]{1,0:T(8,128)(2,1)S(1)}, bf16[256,768]{1,0:T(8,128)(2,1)}, u32[]{:S(2)}) %copy-start.1) | copy-done | bytes 393240
  4.4 0.0 copy-start.2
  4.4 0.9 %copy-done.2 = bf16[8,128,128]{2,1,0:T(8,128)(2,1)S(1)} copy-done((bf16[8,128,128]{2,1,0:T(8,128)(2,1)S(1)}, bf16[8,128,128]{2,1,0:T(8,128)(2,1)}, u32[]{:S(2)}) %copy-start.2) | copy-done | bytes 262168
  5.4 0.0 copy-start.3
  5.4 0.9 %copy-done.3 = bf16[1024,128]{1,0:T(8,128)(2,1)S(1)} copy-done((bf16[1024,128]{1,0:T(8,128)(2,1)S(1)}, bf16[1024,128]{1,0:T(8,128)(2,1)}, u32[]{:S(2)}) %copy-start.3) | copy-done | bytes 262168
  6.3 0.0 copy-start.5
  6.3 0.9 %copy-done.5 = bf16[256,256]{1,0:T(8,128)(2,1)S(1)} copy-done((bf16[256,256]{1,0:T(8,128)(2,1)S(1)}, bf16[256,256]{1,0:T(8,128)(2,1)}, u32[]{:S(2)}) %copy-start.5) | copy-done | bytes 131096
  7.2 0.0 copy-start.6
  7.2 0.9 %copy-done.6 = bf16[256,256]{1,0:T(8,128)(2,1)S(1)} copy-done((bf16[256,256]{1,0:T(8,128)(2,1)S(1)}, bf16[256,256]{1,0:T(8,128)(2,1)}, u32[]{:S(2)}) %copy-start.6) | copy-done | bytes 131096
  8.1 0.0 copy-start.7
  8.1 0.9 %copy-done.7 = bf16[256,256]{1,0:T(8,128)(2,1)S(1)} copy-done((bf16[256,256]{1,0:T(8,128)(2,1)S(1)}, bf16[256,256]{1,0:T(8,128)(2,1)}, u32[]{:S(2)}) %copy-start.7) | copy-done | bytes 131096
  9.0 0.9 %copy-done.8 = bf16[256,256]{1,0:T(8,128)(2,1)S(1)} copy-done((bf16[256,256]{1,0:T(8,128)(2,1)S(1)}, bf16[256,256]{1,0:T(8,128)(2,1)}, u32[]{:S(2)}) %copy-start.8) | copy-done | bytes 131096
  9.9 0.8 %copy-done.9 = bf16[128,256]{1,0:T(8,128)(2,1)S(1)} copy-done((bf16[128,256]{1,0:T(8,128)(2,1)S(1)}, bf16[128,256]{1,0:T(8,128)(2,1)}, u32[]{:S(2)}) %copy-start.9) | copy-done | bytes 65560
  10.8 0.8 %copy-done.10 = bf16[128,256]{1,0:T(8,128)(2,1)S(1)} copy-done((bf16[128,256]{1,0:T(8,128)(2,1)S(1)}, bf16[128,256]{1,0:T(8,128)(2,1)}, u32[]{:S(2)}) %copy-start.10) | copy-done | bytes 65560
  11.6 0.8 copy-done.11
  12.4 0.8 copy-done.12
  13.1 0.7 copy-done.13
  13.8 0.7 copy-done.14
  14.5 64.9 %shard_map.194 = (bf16[32,8,256]{2,1,0:T(8,128)(2,1)S(1)}, bf16[8,128,128]{2,1,0:T(8,128)(2,1)S(1)}) custom-call(bf16[2,128,256]{2,1,0:T(8,128)(2,1)S(1)} %copy-done.4, s32[2,128]{1,0:T(2,128)S(1)} %copy-done.15, s32[1,128]{1,0:T(1,128)S(1)} %bitcast.1, bf16[8,128,128]{2,1,0:T(8,128)(2,1)S(1)} %copy-done.2, s32[8,128]{1,0:T(8,128)S(1)} %copy-done.14, ...), custom_call_target="tpu_custom_call" | custom-call | flops 1000000000 | bytes 3000000 | tf_op jit(solution)/shard_map/pallas_call | solution.py:278
  79.5 0.7 copy.25
  80.1 0.7 copy.26
  (7 shorter events, 0.0 us)
Async XLA Ops:
  0.6 1.8 %copy-start.4 = (bf16[2,128,256]{2,1,0:T(8,128)(2,1)S(1)}, bf16[2,128,256]{2,1,0:T(8,128)(2,1)}, u32[]{:S(2)}) copy-start(bf16[2,128,256]{2,1,0:T(8,128)(2,1)} %act.1) | copy-start | bytes 393220
  1.5 0.9 %copy-start.15 = (s32[2,128]{1,0:T(2,128)S(1)}, s32[2,128]{1,0:T(2,128)}, u32[]{:S(2)}) copy-start(s32[2,128]{1,0:T(2,128)} %ids.1) | copy-start | bytes 3076
  1.5 0.9 %copy-start.16 = (s32[128]{0:T(128)S(1)}, s32[128]{0:T(128)}, u32[]{:S(2)}) copy-start(s32[128]{0:T(128)} %param.21) | copy-start | bytes 1540
  2.4 1.0 %copy-start = (bf16[256,768]{1,0:T(8,128)(2,1)S(1)}, bf16[256,768]{1,0:T(8,128)(2,1)}, u32[]{:S(2)}) copy-start(bf16[256,768]{1,0:T(8,128)(2,1)} %row_kvg.1) | copy-start | bytes 1179652
  3.4 1.0 %copy-start.1 = (bf16[256,768]{1,0:T(8,128)(2,1)S(1)}, bf16[256,768]{1,0:T(8,128)(2,1)}, u32[]{:S(2)}) copy-start(bf16[256,768]{1,0:T(8,128)(2,1)} %col_kvg.1) | copy-start | bytes 1179652
  4.4 0.9 %copy-start.2 = (bf16[8,128,128]{2,1,0:T(8,128)(2,1)S(1)}, bf16[8,128,128]{2,1,0:T(8,128)(2,1)}, u32[]{:S(2)}) copy-start(bf16[8,128,128]{2,1,0:T(8,128)(2,1)} %pair.1) | copy-start | bytes 786436
  5.4 0.9 %copy-start.3 = (bf16[1024,128]{1,0:T(8,128)(2,1)S(1)}, bf16[1024,128]{1,0:T(8,128)(2,1)}, u32[]{:S(2)}) copy-start(bf16[1024,128]{1,0:T(8,128)(2,1)} %opm_w.1) | copy-start | bytes 786436
  6.3 0.9 %copy-start.5 = (bf16[256,256]{1,0:T(8,128)(2,1)S(1)}, bf16[256,256]{1,0:T(8,128)(2,1)}, u32[]{:S(2)}) copy-start(bf16[256,256]{1,0:T(8,128)(2,1)} %row_q.1) | copy-start | bytes 393220
  7.2 0.9 %copy-start.6 = (bf16[256,256]{1,0:T(8,128)(2,1)S(1)}, bf16[256,256]{1,0:T(8,128)(2,1)}, u32[]{:S(2)}) copy-start(bf16[256,256]{1,0:T(8,128)(2,1)} %row_o.1) | copy-start | bytes 393220
  8.1 0.9 %copy-start.7 = (bf16[256,256]{1,0:T(8,128)(2,1)S(1)}, bf16[256,256]{1,0:T(8,128)(2,1)}, u32[]{:S(2)}) copy-start(bf16[256,256]{1,0:T(8,128)(2,1)} %col_q.1) | copy-start | bytes 393220
  9.0 0.9 %copy-start.8 = (bf16[256,256]{1,0:T(8,128)(2,1)S(1)}, bf16[256,256]{1,0:T(8,128)(2,1)}, u32[]{:S(2)}) copy-start(bf16[256,256]{1,0:T(8,128)(2,1)} %col_o.1) | copy-start | bytes 393220
  9.9 0.8 %copy-start.9 = (bf16[128,256]{1,0:T(8,128)(2,1)S(1)}, bf16[128,256]{1,0:T(8,128)(2,1)}, u32[]{:S(2)}) copy-start(bf16[128,256]{1,0:T(8,128)(2,1)} %tri_w.1) | copy-start | bytes 196612
  10.8 0.8 %copy-start.10 = (bf16[128,256]{1,0:T(8,128)(2,1)S(1)}, bf16[128,256]{1,0:T(8,128)(2,1)}, u32[]{:S(2)}) copy-start(bf16[128,256]{1,0:T(8,128)(2,1)} %tri_g.1) | copy-start | bytes 196612
  11.6 0.8 copy-start.11
  12.4 0.8 copy-start.12
  13.1 0.7 copy-start.13
  13.8 0.7 copy-start.14

commit v2 on v1

v2 whole, which is shorter than its diff:
```python
import jax
import jax.numpy as jnp
from jax import lax
from jax.experimental import pallas as pl
from jax.experimental.pallas import tpu as pltpu
from jax.sharding import PartitionSpec as P

N = 16
HEADS = 8
HEAD = 32
INPUTS = 19
F32 = jnp.float32
BF16 = jnp.bfloat16
NN = (((1,), (0,)), ((), ()))
NT = (((1,), (1,)), ((), ()))
TN = (((0,), (0,)), ((), ()))
MESH = pl.DeviceIdType.MESH
OFFSETS = (1, 15, 2, 14, 3, 13, 4, 12, 5, 11, 6, 10, 7, 9, 8)
BIAS, MSA, OPM, TRI, SUM, WIRES = 0, 1, 2, 4, 6, 7


def dot(a, b, dims=NN):
    return lax.dot_general(a, b, dims, preferred_element_type=F32)


def sigmoid(x):
    return 0.5 * jnp.tanh(0.5 * x) + 0.5


def norm(x, axis=-1):
    centred = x - jnp.mean(x, axis=axis, keepdims=True)
    var = jnp.mean(centred * centred, axis=axis, keepdims=True)
    return (centred * lax.rsqrt(var + 1e-05)).astype(BF16)


def iota(shape, axis):
    return lax.broadcasted_iota(jnp.int32, shape, axis)


def ones_where(condition):
    return condition.astype(F32).astype(BF16)


def kernel(*refs):
    n = INPUTS
    body(refs[:n], refs[n], refs[n + 1], refs[n + 2:2 * n + 2], *refs[2 * n + 2:])


def body(
    hbm, msa_out, pair_out, held,
    bias_send, bias_recv, msa_send, msa_recv, opm_send, opm_recv,
    tri_send, tri_recv, sum_send, sum_recv,
    bias_rows, bias_all, table_pad, score, head_ones, xr, w2, wt, lift_x, opm_f, tcat,
    right_f, pair_one, tri_n, gate, xt, zt,
    in_sem, send_sem, recv_sem,
):
    (
        act, ids, present, pair, valid, table,
        row_q, row_kvg, bias_w, row_o, col_q, col_kvg, col_o,
        lift, opm_w, tri_w, tri_g, out_g, out_w,
    ) = held
    loads = {
        id(to): pltpu.make_async_copy(at, to, in_sem.at[n])
        for n, (at, to) in enumerate(zip(hbm, held))
    }
    for ref in (pair, bias_w):
        loads[id(ref)].start()

    me = lax.axis_index("axial")
    peers = {r: lax.rem(me + r, N) for r in OFFSETS}
    barrier = pltpu.get_barrier_semaphore()
    for r in OFFSETS:
        pl.semaphore_signal(
            barrier, inc=1, device_id={"axial": peers[r]}, device_id_type=MESH
        )
    for ref in (
        ids, act, table, row_q, row_kvg, present, row_o, opm_w, lift,
        tri_w, tri_g, col_q, col_kvg, col_o, valid, out_g, out_w,
    ):
        loads[id(ref)].start()

    def need(*refs):
        for ref in refs:
            loads.pop(id(ref)).wait()

    wires = {BIAS: (bias_send, bias_recv)}
    for s in range(1):
        wires[MSA + s] = (msa_send.at[s], msa_recv.at[s])
    for s in range(2):
        wires[OPM + s] = (opm_send.at[s], opm_recv.at[s])
    for s in range(2):
        wires[TRI + s] = (tri_send.at[s], tri_recv.at[s])
    for s in range(1):
        wires[SUM + s] = (sum_send.at[s], sum_recv.at[s])

    def copy(wire, r, src, dst):
        return pltpu.make_async_remote_copy(
            src_ref=src, dst_ref=dst,
            send_sem=send_sem.at[wire], recv_sem=recv_sem.at[wire],
            device_id={"axial": peers[r]}, device_id_type=MESH,
        )

    def outgoing(wire):
        src, dst = wires[wire]
        whole = wire == BIAS or OPM <= wire < TRI
        return [
            copy(wire, r, src if whole else src.at[peers[r]], dst.at[me])
            for r in OFFSETS
        ]

    def send(wire):
        src, dst = wires[wire]
        for c in outgoing(wire):
            c.start()
        whole = wire == BIAS or OPM <= wire < TRI
        dst[me] = src[...] if whole else src[me]

    def finish(wire):
        at = wires[wire][1].at[pl.ds(0, N - 1)]
        copy(wire, 1, at, at).wait_send()

    def await_all(wire):
        at = wires[wire][1].at[pl.ds(0, N - 1)]
        copy(wire, 1, at, at).wait_recv()

    need(pair, bias_w)
    pn = norm(pair[...].astype(F32)).reshape(1024, 128)
    bias_t = dot(bias_w[...], pn, NT)
    for i in range(8):
        bias_rows[pl.ds(i, 8, stride=8), :] = bias_t[:, i * 128:(i + 1) * 128]
    bias_send[...] = bias_rows[...].astype(BF16)
    pl.semaphore_wait(barrier, N - 1)
    send(BIAS)

    need(table, ids, act, row_q, row_kvg)
    head_of = iota((1, 256), 1) // HEAD
    head_mask = [ones_where(head_of == h) for h in range(HEADS)]

    def project(x, wq, wkvg):
        xn = norm(x)
        q = (dot(xn, wq[...]) * HEAD ** -0.5).astype(BF16)
        kvg = dot(xn, wkvg[...])
        return q, kvg[:, :256].astype(BF16), kvg[:, 256:512].astype(BF16), kvg[:, 512:]

    def by_head(a):
        return jnp.concatenate([a * m for m in head_mask], axis=0)

    def mix(scores, extra, v, g):
        parts = []
        for h in range(HEADS):
            one = scores[h * 128:(h + 1) * 128] + extra(h)
            parts.append(jnp.exp(one - jnp.max(one, axis=-1, keepdims=True)).astype(BF16))
        weights = jnp.concatenate(parts, axis=1)
        total = dot(weights, head_ones[...])
        return (dot(weights, by_head(v)) * (sigmoid(g) / total)).astype(BF16)

    table_pad[...] = jnp.zeros((32, 256), F32)
    table_pad[0:23, :] = table[...].astype(F32)
    table_b = table_pad[...].astype(BF16)
    rows = []
    for s in range(2):
        hot = (iota((32, 128), 0) == ids[s:s + 1, :]).astype(F32).T.astype(BF16)
        x = act[s].astype(F32) + dot(hot, table_b)
        q, k, v, g = project(x, row_q, row_kvg)
        score[s] = dot(by_head(q), k, NT)
        rows.append((x, v, g))

    head_ones[...] = ones_where(iota((1024, 256), 0) // 128 == iota((1024, 256), 1) // HEAD)
    need(opm_w, lift, tri_w, tri_g)
    opm_f[...] = opm_w[...].astype(F32)
    for d in range(32):
        w2[:, d * 128:(d + 1) * 128] = opm_f[pl.ds(d, 32, stride=32), :].astype(BF16)
    wt[0:256, :] = tri_w[...].astype(F32).T.astype(BF16)
    wt[256:512, :] = tri_g[...].astype(F32).T.astype(BF16)
    spread = ones_where(iota((64, 1024), 0) == 32 + iota((64, 1024), 1) // 32)
    lift_x[...] = dot(lift[...], spread, TN).astype(BF16)

    need(present, row_o, col_q, col_kvg, col_o, valid, out_g, out_w)
    await_all(BIAS)
    key_bias = 1000000000.0 * (present[...].astype(F32) - 1.0)
    for p in range(N):
        block = bias_recv[p].astype(F32)
        for h in range(HEADS):
            bias_all[h, p * 8:(p + 1) * 8, :] = block[h * 8:(h + 1) * 8] + key_bias
    for s in range(2):
        x, v, g = rows[s]
        heads = mix(score[s], lambda h: bias_all[h], v, g)
        x = x + dot(heads, row_o[...])
        for p in range(N):
            block = x[p * 8:(p + 1) * 8]
            msa_send[0, p, s * 16:(s + 1) * 16, :] = jnp.concatenate([block[:, :128], block[:, 128:]], axis=0).astype(BF16)

    send(MSA)

    await_all(MSA)
    for p in range(N):
        block = msa_recv[0, p].astype(F32)
        for s in range(2):
            at = (p * 2 + s) * 8
            for half in range(2):
                xr[half, at:at + 8, :] = block[(s * 2 + half) * 8:(s * 2 + half + 1) * 8]

    own = jnp.where(iota((128, 128), 0) // 32 == iota((128, 128), 1) // 32, 0.0, -jnp.inf)
    own = own.astype(F32)
    keep = iota((128, 1024), 0) % 32 == iota((128, 1024), 1) % 32
    done = []
    for n in range(2):
        x = jnp.concatenate(
            [
                jnp.concatenate(
                    [xr[half, pl.ds(n * 4 + l, 32, stride=8), :] for l in range(4)], axis=0
                )
                for half in range(2)
            ],
            axis=1,
        )
        q, k, v, g = project(x, col_q, col_kvg)
        heads = mix(dot(by_head(q), k, NT), lambda h: own, v, g)
        z = (x + dot(heads, col_o[...])).astype(BF16).astype(F32)
        zn = norm(z)
        right = dot(zn, lift_x[...])
        right = jnp.where(keep, right, 0.0).astype(BF16)
        total = jnp.zeros((16, 256), F32)
        for a in range(4):
            pick = ones_where(iota((16, 128), 0) == a * 4 + iota((16, 128), 1) // 32)
            total += dot(pick, right[:, a * 256:(a + 1) * 256])
        opm_send[n] = total.astype(BF16)
        send(OPM + n)
        done.append((z, zn))

    for n in range(2):
        z = done[n][0]
        for half in range(2):
            for l in range(4):
                xr[half, pl.ds(n * 4 + l, 32, stride=8), :] = z[
                    l * 32:(l + 1) * 32, half * 128:(half + 1) * 128
                ]
    for half in range(2):
        msa_out[:, :, half * 128:(half + 1) * 128] = xr[half].reshape(32, 8, 128).astype(BF16)
    zn = jnp.concatenate([done[0][1], done[1][1]], axis=0)
    left = dot(zn, lift[0:32, :], NT).astype(BF16)
    for d in range(0, 32, 2):
        t = dot(left, w2[:, d * 128:(d + 2) * 128]).astype(BF16)
        for i in range(8):
            for e in range(2):
                tcat[(d + e) * 32:(d + e + 1) * 32, i * 128:(i + 1) * 128] = t[
                    i * 32:(i + 1) * 32, e * 128:(e + 1) * 128
                ]

    for n in range(2):
        await_all(OPM + n)
        for p in range(N):
            block = opm_recv[n, p].astype(F32)
            at = p * 8 + n * 4
            for a in range(4):
                right_f[at:at + 4, a * 256:(a + 1) * 256] = block[a * 4:(a + 1) * 4]
    right = right_f[...].astype(BF16)

    for n in range(4):
        update = dot(right, tcat[:, n * 256:(n + 1) * 256])
        for e in range(2):
            i = n * 2 + e
            one = pair[i].astype(F32) + update[:, e * 128:(e + 1) * 128] * (1.0 / 32)
            pair_one[i] = one
            tn = norm(one)
            tri_n[i] = tn
            both = dot(wt[...], tn, NT)
            both = sigmoid(both[256:]) * both[:256] * valid[i:i + 1, :].astype(F32)
            for p in range(N):
                block = jnp.concatenate(
                    [both[p * 8:(p + 1) * 8], both[128 + p * 8:128 + (p + 1) * 8]], axis=0
                )
                tri_send[n // 2, p, :, (n % 2 * 2 + e) * 128:(n % 2 * 2 + e + 1) * 128] = block.astype(BF16)
        if n % 2 == 1:
            send(TRI + n // 2)
    for i in range(8):
        gate[i] = sigmoid(dot(tri_n[i], out_g[...]))
    for n in range(2):
        await_all(TRI + n)
        for p in range(N):
            block = tri_recv[n, p].astype(F32)
            for e in range(4):
                at = (p * 8 + n * 4 + e) * 16
                xt[at:at + 16, :] = block[:, e * 128:(e + 1) * 128]

    for n in range(1):
        sums = []
        for c in range(n * 8, (n + 1) * 8):
            a = xt[pl.ds(c, 128, stride=16), :].astype(BF16)
            b = xt[pl.ds(8 + c, 128, stride=16), :].astype(BF16)
            sums.append(dot(a, b, NT))
        for p in range(N):
            sum_send[n, p] = jnp.concatenate(
                [s[p * 8:(p + 1) * 8] for s in sums], axis=0
            ).astype(BF16)
        send(SUM + n)
    for n in range(1):
        await_all(SUM + n)
        for p in range(N):
            at = (p * 8 + n * 8) * 8
            zt[at:at + 64, :] = sum_recv[n, p].astype(F32)

    for i in range(8):
        mixed = norm(zt[pl.ds(i, 128, stride=8), :], axis=0)
        update = dot(mixed, out_w[...], TN)
        pair_out[i] = (pair_one[i] + gate[i] * update).astype(BF16)
    for wire in wires:
        finish(wire)


def local(*args):
    hbm = pl.BlockSpec(memory_space=pl.ANY)
    vmem = pl.BlockSpec(memory_space=pltpu.VMEM)
    args = list(args)
    args[2] = args[2].reshape(1, 128)
    args[8] = args[8].T
    args[13] = args[13].T
    shapes = (
        jax.ShapeDtypeStruct((32, 8, 256), BF16),
        jax.ShapeDtypeStruct((8, 128, 128), BF16),
    )
    return pl.pallas_call(
        kernel,
        out_shape=shapes,
        in_specs=[hbm] * len(args),
        out_specs=(vmem, vmem),
        scratch_shapes=[pltpu.VMEM(a.shape, a.dtype) for a in args] + [
            pltpu.VMEM((64, 128), BF16),
            pltpu.VMEM((N, 64, 128), BF16),
            pltpu.VMEM((1, N, 32, 128), BF16),
            pltpu.VMEM((1, N, 32, 128), BF16),
            pltpu.VMEM((2, 16, 256), BF16),
            pltpu.VMEM((2, N, 16, 256), BF16),
            pltpu.VMEM((2, N, 16, 512), BF16),
            pltpu.VMEM((2, N, 16, 512), BF16),
            pltpu.VMEM((1, N, 64, 128), BF16),
            pltpu.VMEM((1, N, 64, 128), BF16),
            pltpu.VMEM((64, 128), F32),
            pltpu.VMEM((HEADS, 128, 128), F32),
            pltpu.VMEM((32, 256), F32),
            pltpu.VMEM((2, 1024, 128), F32),
            pltpu.VMEM((1024, 256), BF16),
            pltpu.VMEM((2, 256, 128), F32),
            pltpu.VMEM((32, 4096), BF16),
            pltpu.VMEM((512, 128), BF16),
            pltpu.VMEM((256, 1024), BF16),
            pltpu.VMEM((1024, 128), F32),
            pltpu.VMEM((1024, 1024), BF16),
            pltpu.VMEM((128, 1024), F32),
            pltpu.VMEM((8, 128, 128), F32),
            pltpu.VMEM((8, 128, 128), BF16),
            pltpu.VMEM((8, 128, 128), F32),
            pltpu.VMEM((2048, 128), F32),
            pltpu.VMEM((1024, 128), F32),
            pltpu.SemaphoreType.DMA((INPUTS,)),
            pltpu.SemaphoreType.DMA((WIRES,)),
            pltpu.SemaphoreType.DMA((WIRES,)),
        ],
        compiler_params=pltpu.CompilerParams(
            collective_id=0, has_side_effects=True, vmem_limit_bytes=60 * 1024 * 1024,
        ),
        cost_estimate=pl.CostEstimate(
            flops=10**9, bytes_accessed=3 * 10**6, transcendentals=10**6
        ),
    )(*args)


def solution(mesh):
    rows = P(("dp", "axial"))
    return jax.shard_map(
        local,
        mesh=mesh,
        in_specs=(rows, rows, P("dp"), rows, rows) + (P(),) * 14,
        out_specs=(P("dp", "axial", None), rows),
        check_vma=False,
    )
```

time: 81.5 us -> 61.7 us (0.76)
  local copies, waits for them, and re-layouts: 15.2 us -> 2.32 us
  Pallas kernels: 64.9 us -> 58.4 us
    unnamed x38 -> x4, local copies, waits for them, and re-layouts: 15.2 us -> 2.32 us
    pallas_call x1, Pallas kernels: 64.9 us -> 58.4 us  [local(): pl.pallas_call(kernel, out_shape=shapes, in_specs=[hbm] * len(args), out_...]
where the time goes in v2:
time: 61.7 us; the launch traced here: 61.4 us
  Pallas kernels  58.4 us (95%)
  local copies, waits for them, and re-layouts  2.32 us (4%)
  between operations  0.66 us (1%)
    pallas_call x1, Pallas kernels, local(): pl.pallas_call(kernel, out_shape=shapes, in_specs=[hbm] * len(args), out_...  58.4 us
    unnamed x4, local copies, waits for them, and re-layouts  2.32 us

profile of v2, /device:TPU:16, one launch (start us, length us, event | category | flops | bytes accessed | tf_op | source)
XLA Modules:
  0.0 61.4 jit_solution(7111481757638445701)
XLA Ops:
  0.6 58.4 %shard_map.194 = (bf16[32,8,256]{2,1,0:T(8,128)(2,1)}, bf16[8,128,128]{2,1,0:T(8,128)(2,1)}) custom-call(bf16[2,128,256]{2,1,0:T(8,128)(2,1)} %refs_0_.1, s32[2,128]{1,0:T(2,128)} %refs_1_.1, s32[1,128]{1,0:T(1,128)} %bitcast.5, bf16[8,128,128]{2,1,0:T(8,128)(2,1)} %refs_3_.1, s32[8,128]{1,0:T(8,128)} %refs_4_.1, bf16[23,256]{1,0:T(8,128)(2,1)} %refs_5_.1, ...), custom_call_target="tpu_custom_call" | custom-call | flops 1000000000 | bytes 3000000 | tf_op jit(solution)/shard_map/pallas_call | solution.py:322
  59.1 0.0 copy-start
  59.1 1.6 %copy.23 = bf16[32,8,256]{2,1,0:T(8,128)(2,1)} copy(bf16[32,8,256]{2,1,0:T(8,128)(2,1)} %get-tuple-element.4) | data formatting | bytes 262144
  60.7 0.0 copy-done
  60.7 0.7 %copy.24 = bf16[8,128,128]{2,1,0:T(8,128)(2,1)} copy(bf16[8,128,128]{2,1,0:T(8,128)(2,1)S(1)} %copy-done) | data formatting | bytes 524288
Async XLA Ops:
  59.1 1.6 %copy-start = (bf16[8,128,128]{2,1,0:T(8,128)(2,1)S(1)}, bf16[8,128,128]{2,1,0:T(8,128)(2,1)}, u32[]{:S(2)}) copy-start(bf16[8,128,128]{2,1,0:T(8,128)(2,1)} %get-tuple-element.5) | copy-start | bytes 786436

commit v3 on v2

--- a/solution.py
+++ b/solution.py
@@ -15,8 +15,9 @@
 NT = (((1,), (1,)), ((), ()))
 TN = (((0,), (0,)), ((), ()))
 MESH = pl.DeviceIdType.MESH
-OFFSETS = (1, 15, 2, 14, 3, 13, 4, 12, 5, 11, 6, 10, 7, 9, 8)
-BIAS, MSA, OPM, TRI, SUM, WIRES = 0, 1, 2, 4, 6, 7
+NEAR, FAR = (1, 15, 2, 14, 3, 13, 4), (12, 5, 11, 6, 10, 7, 9, 8)
+OFFSETS = NEAR + FAR
+BIAS, MSA, OPM, TRI, SUM, WIRES = 0, 2, 3, 5, 7, 8
 
 
 def dot(a, b, dims=NN):
@@ -49,8 +50,8 @@
 def body(
     hbm, msa_out, pair_out, held,
     bias_send, bias_recv, msa_send, msa_recv, opm_send, opm_recv,
-    tri_send, tri_recv, sum_send, sum_recv,
-    bias_rows, bias_all, table_pad, score, head_ones, xr, w2, wt, lift_x, opm_f, tcat,
+    first_send, first_recv, tri_send, tri_recv, sum_send, sum_recv,
+    bias_rows, row_x, row_gate, row_v, table_pad, score, head_ones, xr, w2, wt, lift_x, opm_f, tcat,
     right_f, pair_one, tri_n, gate, xt, zt,
     in_sem, send_sem, recv_sem,
 ):
@@ -83,13 +84,13 @@
         for ref in refs:
             loads.pop(id(ref)).wait()
 
-    wires = {BIAS: (bias_send, bias_recv)}
+    wires = {BIAS: (bias_send, bias_recv), BIAS + 1: (bias_send, bias_recv)}
+    offsets = {BIAS: NEAR, BIAS + 1: FAR}
     for s in range(1):
         wires[MSA + s] = (msa_send.at[s], msa_recv.at[s])
     for s in range(2):
         wires[OPM + s] = (opm_send.at[s], opm_recv.at[s])
-    for s in range(2):
-        wires[TRI + s] = (tri_send.at[s], tri_recv.at[s])
+    wires[TRI], wires[TRI + 1] = (first_send, first_recv), (tri_send, tri_recv)
     for s in range(1):
         wires[SUM + s] = (sum_send.at[s], sum_recv.at[s])
 
@@ -102,25 +103,26 @@
 
     def outgoing(wire):
         src, dst = wires[wire]
-        whole = wire == BIAS or OPM <= wire < TRI
+        whole = BIAS <= wire < MSA or OPM <= wire < TRI
         return [
             copy(wire, r, src if whole else src.at[peers[r]], dst.at[me])
-            for r in OFFSETS
+            for r in offsets.get(wire, OFFSETS)
         ]
 
     def send(wire):
         src, dst = wires[wire]
         for c in outgoing(wire):
             c.start()
-        whole = wire == BIAS or OPM <= wire < TRI
-        dst[me] = src[...] if whole else src[me]
+        whole = BIAS <= wire < MSA or OPM <= wire < TRI
+        if wire != BIAS + 1:
+            dst[me] = src[...] if whole else src[me]
 
     def finish(wire):
-        at = wires[wire][1].at[pl.ds(0, N - 1)]
+        at = wires[wire][1].at[pl.ds(0, len(offsets.get(wire, OFFSETS)))]
         copy(wire, 1, at, at).wait_send()
 
     def await_all(wire):
-        at = wires[wire][1].at[pl.ds(0, N - 1)]
+        at = wires[wire][1].at[pl.ds(0, len(offsets.get(wire, OFFSETS)))]
         copy(wire, 1, at, at).wait_recv()
 
     need(pair, bias_w)
@@ -131,6 +133,7 @@
     bias_send[...] = bias_rows[...].astype(BF16)
     pl.semaphore_wait(barrier, N - 1)
     send(BIAS)
+    send(BIAS + 1)
 
     need(table, ids, act, row_q, row_kvg)
     head_of = iota((1, 256), 1) // HEAD
@@ -157,40 +160,67 @@
     table_pad[...] = jnp.zeros((32, 256), F32)
     table_pad[0:23, :] = table[...].astype(F32)
     table_b = table_pad[...].astype(BF16)
-    rows = []
     for s in range(2):
-        hot = (iota((32, 128), 0) == ids[s:s + 1, :]).astype(F32).T.astype(BF16)
+        hot = (iota((32, 1), 0) == ids[s:s + 1, :]).astype(F32).T.astype(BF16)
         x = act[s].astype(F32) + dot(hot, table_b)
         q, k, v, g = project(x, row_q, row_kvg)
         score[s] = dot(by_head(q), k, NT)
-        rows.append((x, v, g))
-
-    head_ones[...] = ones_where(iota((1024, 256), 0) // 128 == iota((1024, 256), 1) // HEAD)
+        row_x[s], row_gate[s], row_v[s] = x, sigmoid(g), by_head(v)
+
+    head_ones[...] = ones_where(iota((1024, 1), 0) // 128 == iota((1, 256), 1) // HEAD)
     need(opm_w, lift, tri_w, tri_g)
     opm_f[...] = opm_w[...].astype(F32)
     for d in range(32):
         w2[:, d * 128:(d + 1) * 128] = opm_f[pl.ds(d, 32, stride=32), :].astype(BF16)
     wt[0:256, :] = tri_w[...].astype(F32).T.astype(BF16)
     wt[256:512, :] = tri_g[...].astype(F32).T.astype(BF16)
-    spread = ones_where(iota((64, 1024), 0) == 32 + iota((64, 1024), 1) // 32)
+    spread = ones_where(iota((64, 1), 0) == 32 + iota((1, 1024), 1) // 32)
     lift_x[...] = dot(lift[...], spread, TN).astype(BF16)
 
     need(present, row_o, col_q, col_kvg, col_o, valid, out_g, out_w)
-    await_all(BIAS)
     key_bias = 1000000000.0 * (present[...].astype(F32) - 1.0)
-    for p in range(N):
-        block = bias_recv[p].astype(F32)
-        for h in range(HEADS):
-            bias_all[h, p * 8:(p + 1) * 8, :] = block[h * 8:(h + 1) * 8] + key_bias
-    for s in range(2):
-        x, v, g = rows[s]
-        heads = mix(score[s], lambda h: bias_all[h], v, g)
+    for group in ((0,) + NEAR, FAR):
+        await_all(BIAS if group[0] == 0 else BIAS + 1)
+        owners = [peers[N - r] if r else me for r in group]
+        biases = [bias_recv[p].astype(F32) for p in owners]
+        many = len(owners) * 8
+
+        def rows_of(ref, s):
+            return jnp.concatenate(
+                [ref[s, pl.ds(pl.multiple_of(p * 8, 8), 8), :] for p in owners], axis=0
+            )
+
+        weights = []
+        for s in range(2):
+            parts = []
+            for h in range(HEADS):
+                one = jnp.concatenate(
+                    [
+                        score[s, pl.ds(pl.multiple_of(h * 128 + p * 8, 8), 8), :]
+                        + (bias[h * 8:(h + 1) * 8] + key_bias)
+                        for p, bias in zip(owners, biases)
+                    ],
+                    axis=0,
+                )
+                parts.append(jnp.exp(one - jnp.max(one, axis=-1, keepdims=True)).astype(BF16))
+            weights.append(jnp.concatenate(parts, axis=1))
+        total = dot(jnp.concatenate(weights, axis=0), head_ones[...])
+        mixed = jnp.concatenate([dot(weights[s], row_v[s]) for s in range(2)], axis=0)
+        gates = jnp.concatenate([rows_of(row_gate, s) for s in range(2)], axis=0)
+        heads = (mixed * (gates / total)).astype(BF16)
+        x = jnp.concatenate([rows_of(row_x, s) for s in range(2)], axis=0)
         x = x + dot(heads, row_o[...])
-        for p in range(N):
-            block = x[p * 8:(p + 1) * 8]
-            msa_send[0, p, s * 16:(s + 1) * 16, :] = jnp.concatenate([block[:, :128], block[:, 128:]], axis=0).astype(BF16)
-
-    send(MSA)
+        for n, p in enumerate(owners):
+            at = (n * 8, n * 8 + many)
+            msa_send[0, p] = jnp.concatenate(
+                [x[a:a + 8, half * 128:(half + 1) * 128] for a in at for half in range(2)],
+                axis=0,
+            ).astype(BF16)
+        for r, p in zip(group, owners):
+            if r:
+                copy(MSA, N - r, msa_send.at[0, p], msa_recv.at[0, me]).start()
+            else:
+                msa_recv[0, me] = msa_send[0, me]
 
     await_all(MSA)
     for p in range(N):
@@ -200,9 +230,9 @@
             for half in range(2):
                 xr[half, at:at + 8, :] = block[(s * 2 + half) * 8:(s * 2 + half + 1) * 8]
 
-    own = jnp.where(iota((128, 128), 0) // 32 == iota((128, 128), 1) // 32, 0.0, -jnp.inf)
+    own = jnp.where(iota((128, 1), 0) // 32 == iota((1, 128), 1) // 32, 0.0, -jnp.inf)
     own = own.astype(F32)
-    keep = iota((128, 1024), 0) % 32 == iota((128, 1024), 1) % 32
+    keep = iota((128, 1), 0) % 32 == iota((1, 1024), 1) % 32
     done = []
     for n in range(2):
         x = jnp.concatenate(
@@ -222,7 +252,7 @@
         right = jnp.where(keep, right, 0.0).astype(BF16)
         total = jnp.zeros((16, 256), F32)
         for a in range(4):
-            pick = ones_where(iota((16, 128), 0) == a * 4 + iota((16, 128), 1) // 32)
+            pick = ones_where(iota((16, 1), 0) == a * 4 + iota((1, 128), 1) // 32)
             total += dot(pick, right[:, a * 256:(a + 1) * 256])
         opm_send[n] = total.astype(BF16)
         send(OPM + n)
@@ -270,17 +300,21 @@
                 block = jnp.concatenate(
                     [both[p * 8:(p + 1) * 8], both[128 + p * 8:128 + (p + 1) * 8]], axis=0
                 )
-                tri_send[n // 2, p, :, (n % 2 * 2 + e) * 128:(n % 2 * 2 + e + 1) * 128] = block.astype(BF16)
-        if n % 2 == 1:
-            send(TRI + n // 2)
+                if n == 0:
+                    first_send[p, :, i * 128:(i + 1) * 128] = block.astype(BF16)
+                else:
+                    tri_send[p, :, (i - 2) * 128:(i - 1) * 128] = block.astype(BF16)
+        if n == 0:
+            send(TRI)
+    send(TRI + 1)
     for i in range(8):
         gate[i] = sigmoid(dot(tri_n[i], out_g[...]))
-    for n in range(2):
+    for n, (ref, rows) in enumerate(((first_recv, range(2)), (tri_recv, range(2, 8)))):
         await_all(TRI + n)
         for p in range(N):
-            block = tri_recv[n, p].astype(F32)
-            for e in range(4):
-                at = (p * 8 + n * 4 + e) * 16
+            block = ref[p].astype(F32)
+            for e, i in enumerate(rows):
+                at = (p * 8 + i) * 16
                 xt[at:at + 16, :] = block[:, e * 128:(e + 1) * 128]
 
     for n in range(1):
@@ -316,8 +350,8 @@
     args[8] = args[8].T
     args[13] = args[13].T
     shapes = (
-        jax.ShapeDtypeStruct((32, 8, 256), BF16),
-        jax.ShapeDtypeStruct((8, 128, 128), BF16),
+        pltpu.VMEM((32, 8, 256), BF16),
+        pltpu.VMEM((8, 128, 128), BF16),
     )
     return pl.pallas_call(
         kernel,
@@ -331,12 +365,16 @@
             pltpu.VMEM((1, N, 32, 128), BF16),
             pltpu.VMEM((2, 16, 256), BF16),
             pltpu.VMEM((2, N, 16, 256), BF16),
-            pltpu.VMEM((2, N, 16, 512), BF16),
-            pltpu.VMEM((2, N, 16, 512), BF16),
+            pltpu.VMEM((N, 16, 256), BF16),
+            pltpu.VMEM((N, 16, 256), BF16),
+            pltpu.VMEM((N, 16, 768), BF16),
+            pltpu.VMEM((N, 16, 768), BF16),
             pltpu.VMEM((1, N, 64, 128), BF16),
             pltpu.VMEM((1, N, 64, 128), BF16),
             pltpu.VMEM((64, 128), F32),
-            pltpu.VMEM((HEADS, 128, 128), F32),
+            pltpu.VMEM((2, 128, 256), F32),
+            pltpu.VMEM((2, 128, 256), F32),
+            pltpu.VMEM((2, 1024, 256), BF16),
             pltpu.VMEM((32, 256), F32),
             pltpu.VMEM((2, 1024, 128), F32),
             pltpu.VMEM((1024, 256), BF16),

time: 61.7 us -> 59.7 us (0.968)
  Pallas kernels: 58.4 us -> 57.2 us
  local copies, waits for them, and re-layouts: 2.32 us -> 1.36 us
    pallas_call x1, Pallas kernels: 58.4 us -> 57.2 us  [local(): pl.pallas_call(kernel, out_shape=shapes, in_specs=[hbm] * len(args), out_...]
    unnamed x4 -> x2, local copies, waits for them, and re-layouts: 2.32 us -> 1.36 us
where the time goes in v3:
time: 59.7 us; the launch traced here: 59.2 us
  Pallas kernels  57.2 us (96%)
  local copies, waits for them, and re-layouts  1.36 us (2%)
  between operations  0.65 us (1%)
    pallas_call x1, Pallas kernels, local(): pl.pallas_call(kernel, out_shape=shapes, in_specs=[hbm] * len(args), out_...  57.2 us
    unnamed x2, local copies, waits for them, and re-layouts  1.36 us

profile of v3, /device:TPU:16, one launch (start us, length us, event | category | flops | bytes accessed | tf_op | source)
XLA Modules:
  0.0 59.2 jit_solution(11172631514106802989)
XLA Ops:
  0.6 57.2 %shard_map.194 = (bf16[32,8,256]{2,1,0:T(8,128)(2,1)S(1)}, bf16[8,128,128]{2,1,0:T(8,128)(2,1)S(1)}) custom-call(bf16[2,128,256]{2,1,0:T(8,128)(2,1)} %refs_0_.1, s32[2,128]{1,0:T(2,128)} %refs_1_.1, s32[1,128]{1,0:T(1,128)} %bitcast.5, bf16[8,128,128]{2,1,0:T(8,128)(2,1)} %refs_3_.1, s32[8,128]{1,0:T(8,128)} %refs_4_.1, bf16[23,256]{1,0:T(8,128)(2,1)} %refs_5_.1, ...), custom_call_target="tpu_custom_call" | custom-call | flops 1000000000 | bytes 3000000 | tf_op jit(solution)/shard_map/pallas_call | solution.py:356
  57.9 0.7 %copy.23 = bf16[32,8,256]{2,1,0:T(8,128)(2,1)} copy(bf16[32,8,256]{2,1,0:T(8,128)(2,1)S(1)} %get-tuple-element.2) | data formatting | bytes 262144
  58.5 0.7 %copy.24 = bf16[8,128,128]{2,1,0:T(8,128)(2,1)} copy(bf16[8,128,128]{2,1,0:T(8,128)(2,1)S(1)} %get-tuple-element.3) | data formatting | bytes 524288

commit v4 on v3

--- a/solution.py
+++ b/solution.py
@@ -15,7 +15,7 @@
 NT = (((1,), (1,)), ((), ()))
 TN = (((0,), (0,)), ((), ()))
 MESH = pl.DeviceIdType.MESH
-NEAR, FAR = (1, 15, 2, 14, 3, 13, 4), (12, 5, 11, 6, 10, 7, 9, 8)
+NEAR, FAR = (1, 15, 2, 14, 3, 13, 4), (8, 9, 7, 10, 6, 11, 5, 12)
 OFFSETS = NEAR + FAR
 BIAS, MSA, OPM, TRI, SUM, WIRES = 0, 2, 3, 5, 7, 8
 
@@ -85,7 +85,8 @@
             loads.pop(id(ref)).wait()
 
     wires = {BIAS: (bias_send, bias_recv), BIAS + 1: (bias_send, bias_recv)}
-    offsets = {BIAS: NEAR, BIAS + 1: FAR}
+    far_first = (8, 9, 7, 10, 6, 11, 5, 12, 4, 13, 3, 14, 2, 15, 1)
+    offsets = {BIAS: NEAR, BIAS + 1: FAR, OPM: far_first, OPM + 1: far_first, TRI + 1: far_first}
     for s in range(1):
         wires[MSA + s] = (msa_send.at[s], msa_recv.at[s])
     for s in range(2):

time: 59.7 us -> 59.1 us (0.990)
  Pallas kernels: 57.2 us -> 56.6 us
    pallas_call x1, Pallas kernels: 57.2 us -> 56.6 us  [local(): pl.pallas_call(kernel, out_shape=shapes, in_specs=[hbm] * len(args), out_...]
where the time goes in v4:
time: 59.1 us; the launch traced here: 58.6 us
  Pallas kernels  56.6 us (96%)
  local copies, waits for them, and re-layouts  1.36 us (2%)
  between operations  0.65 us (1%)
    pallas_call x1, Pallas kernels, local(): pl.pallas_call(kernel, out_shape=shapes, in_specs=[hbm] * len(args), out_...  56.6 us
    unnamed x2, local copies, waits for them, and re-layouts  1.36 us

profile of v4, /device:TPU:16, one launch (start us, length us, event | category | flops | bytes accessed | tf_op | source)
XLA Modules:
  0.0 58.6 jit_solution(10444492175050694573)
XLA Ops:
  0.6 56.6 %shard_map.194 = (bf16[32,8,256]{2,1,0:T(8,128)(2,1)S(1)}, bf16[8,128,128]{2,1,0:T(8,128)(2,1)S(1)}) custom-call(bf16[2,128,256]{2,1,0:T(8,128)(2,1)} %refs_0_.1, s32[2,128]{1,0:T(2,128)} %refs_1_.1, s32[1,128]{1,0:T(1,128)} %bitcast.5, bf16[8,128,128]{2,1,0:T(8,128)(2,1)} %refs_3_.1, s32[8,128]{1,0:T(8,128)} %refs_4_.1, bf16[23,256]{1,0:T(8,128)(2,1)} %refs_5_.1, ...), custom_call_target="tpu_custom_call" | custom-call | flops 1000000000 | bytes 3000000 | tf_op jit(solution)/shard_map/pallas_call | solution.py:357
  57.2 0.7 %copy.23 = bf16[32,8,256]{2,1,0:T(8,128)(2,1)} copy(bf16[32,8,256]{2,1,0:T(8,128)(2,1)S(1)} %get-tuple-element.2) | data formatting | bytes 262144
  57.9 0.7 %copy.24 = bf16[8,128,128]{2,1,0:T(8,128)(2,1)} copy(bf16[8,128,128]{2,1,0:T(8,128)(2,1)S(1)} %get-tuple-element.3) | data formatting | bytes 524288

commit v5 on v4

--- a/solution.py
+++ b/solution.py
@@ -70,7 +70,7 @@
     me = lax.axis_index("axial")
     peers = {r: lax.rem(me + r, N) for r in OFFSETS}
     barrier = pltpu.get_barrier_semaphore()
-    for r in OFFSETS:
+    for r in OFFSETS[::-1]:
         pl.semaphore_signal(
             barrier, inc=1, device_id={"axial": peers[r]}, device_id_type=MESH
         )

time: 59.1 us -> 58.8 us (level)
  no operation moved by 1% of the time
where the time goes in v5:
time: 58.8 us; the launch traced here: 58.6 us
  Pallas kernels  56.6 us (96%)
  local copies, waits for them, and re-layouts  1.36 us (2%)
  between operations  0.65 us (1%)
    pallas_call x1, Pallas kernels, local(): pl.pallas_call(kernel, out_shape=shapes, in_specs=[hbm] * len(args), out_...  56.6 us
    unnamed x2, local copies, waits for them, and re-layouts  1.36 us

profile of v5, /device:TPU:16, one launch (start us, length us, event | category | flops | bytes accessed | tf_op | source)
XLA Modules:
  0.0 58.6 jit_solution(7155032799570342292)
XLA Ops:
  0.6 56.6 %shard_map.194 = (bf16[32,8,256]{2,1,0:T(8,128)(2,1)S(1)}, bf16[8,128,128]{2,1,0:T(8,128)(2,1)S(1)}) custom-call(bf16[2,128,256]{2,1,0:T(8,128)(2,1)} %refs_0_.1, s32[2,128]{1,0:T(2,128)} %refs_1_.1, s32[1,128]{1,0:T(1,128)} %bitcast.5, bf16[8,128,128]{2,1,0:T(8,128)(2,1)} %refs_3_.1, s32[8,128]{1,0:T(8,128)} %refs_4_.1, bf16[23,256]{1,0:T(8,128)(2,1)} %refs_5_.1, ...), custom_call_target="tpu_custom_call" | custom-call | flops 1000000000 | bytes 3000000 | tf_op jit(solution)/shard_map/pallas_call | solution.py:357
  57.2 0.7 %copy.23 = bf16[32,8,256]{2,1,0:T(8,128)(2,1)} copy(bf16[32,8,256]{2,1,0:T(8,128)(2,1)S(1)} %get-tuple-element.2) | data formatting | bytes 262144
  57.9 0.7 %copy.24 = bf16[8,128,128]{2,1,0:T(8,128)(2,1)} copy(bf16[8,128,128]{2,1,0:T(8,128)(2,1)S(1)} %get-tuple-element.3) | data formatting | bytes 524288
